TPU v7x, 32 devices: a whole 2x2x4 slice. The times are simulated.
32 devices in a mesh: mp: 2 (over x), row: 16 (over z, y, core).
Axes of the slice: x: 2, y: 2, z: 4, core: 2. Of those that a mesh axis runs over, the one named last changes fastest.
Arguments:
- radial_funcs: bfloat16 [128, 1024], P('row'), may hold values from -6 to 6
- kernels: bfloat16 [80, 1024], P('mp'), parts along dimension 0, may hold values from -0.0010299683 to 0.0010299683
- wigner: float32 [40, 128], replicated, may hold values from -4 to 4
- sources: bfloat16 [64, 2048], P('mp', 'row'), parts along dimension 0, may hold values from -6 to 6
- wigner_slots: int32 [2048], P('row'), may hold values from 0 to 127
- owners: int32 [2048], P('row'), may hold values from 0 to 7, as said below
- degrees: int32 [128], P('row'), may hold values from 0 to 30
- frequencies: float32 [2048], P('row'), may hold values from 0.5 to 2
Outputs:
- response: float32 [64, 2048], P('mp', 'row'), parts along dimension 0
There are 2 independent parts, one for each index of `mp`. A program takes and returns all parts, laid end to end along the dimension named above; an argument that names none is the same for every part. Nothing has to cross between parts.
Inputs may be any that keep to these rules, and one draw needn't show every extreme that they name: Within each aligned block of 128 singlets, owners never falls and every value 0 to 7 occurs.
All inputs are finite; a program needn't handle non-finite values.
Results may differ from a plain program's by a relative error of at most 0.0055.
Values may be sent and summed in bfloat16 or wider, within the bound.
A program may use at most 128 MiB of HBM per device.

v0:
```python
import jax
import jax.numpy as jnp
from jax import lax
from jax.sharding import PartitionSpec as P


def lookup(wigner, slot_block):
    return jnp.take(wigner, slot_block, axis=1)


def project(source_block, slot_block, owner_block, wigner, mult_dev):
    angular = lookup(wigner, slot_block)
    member = (owner_block[:, None] == jnp.arange(mult_dev, dtype=jnp.int32)[None, :]).astype(
        jnp.float32
    )
    scaled = angular[:, None, :] * source_block.astype(jnp.float32)[None, :, :]
    return jnp.einsum("skj,ja->ska", scaled, member, precision=lax.Precision.HIGHEST)


def selection(near_deg, far_deg, num_degree):
    level = jnp.arange(num_degree, dtype=jnp.int32)[:, None, None]
    total_deg = near_deg[None, :, None] + far_deg[None, None, :]
    diff_deg = jnp.abs(near_deg[None, :, None] - far_deg[None, None, :])
    return (diff_deg <= level) & (level <= total_deg) & ((total_deg + level) % 2 == 0)


def local(radial_funcs, kernels, wigner, sources, wigner_slots, owners, degrees, frequencies):
    num_degree = kernels.shape[0]
    mult_dev = radial_funcs.shape[0]
    own_part = project(sources, wigner_slots, owners, wigner, mult_dev).astype(jnp.bfloat16)
    projected, deg_all = (
        lax.all_gather(own_part, "row", axis=2, tiled=True),
        lax.all_gather(degrees, "row", axis=0, tiled=True),
    )
    weighted = (
        radial_funcs.astype(jnp.float32)[None] * kernels.astype(jnp.float32)[:, None, :]
    ).astype(jnp.bfloat16)
    weighted = weighted.reshape(num_degree * mult_dev, radial_funcs.shape[1])
    fetched = lax.all_gather(radial_funcs, "row", axis=0, tiled=True)
    piece_rows = fetched.shape[0]
    integral = lax.dot_general(
        weighted, fetched, (((1,), (1,)), ((), ())), preferred_element_type=jnp.float32
    )
    integral = integral.reshape(num_degree, mult_dev, piece_rows)
    kept_block = jnp.where(
        selection(degrees, deg_all, num_degree), integral, jnp.float32(0.0)
    ).astype(jnp.bfloat16)
    coupled = jnp.einsum("sab,skb->ska", kept_block, projected, preferred_element_type=jnp.float32)
    angular = lookup(wigner, wigner_slots)
    member = (owners[None, :] == jnp.arange(mult_dev, dtype=jnp.int32)[:, None]).astype(jnp.float32)
    spread = jnp.einsum("ska,ai->ski", coupled, member, precision=lax.Precision.HIGHEST)
    return frequencies[None, :] * sources.astype(jnp.float32) + jnp.sum(
        angular[:, None, :] * spread, axis=0
    )


def solution(mesh):
    in_specs = (
        P("row", None),
        P("mp", None),
        P(),
        P("mp", "row"),
        P("row"),
        P("row"),
        P("row"),
        P("row"),
    )
    out_specs = P("mp", "row")
    return jax.shard_map(local, mesh=mesh, in_specs=in_specs, out_specs=out_specs, check_vma=False)
```

profile of v0, /device:TPU:0, one launch (start us, length us, event | category | flops | bytes accessed | tf_op | source)
XLA Modules:
  0.0 67.7 jit_solution(15264262395300003951)
XLA Ops:
  0.0 0.8 %copy.11 = f32[40,128]{0,1:T(8,128)S(1)} copy(f32[40,128]{1,0:T(8,128)} %param.12) | data formatting | bytes 40960 | tf_op args[2]
  0.8 0.7 compare_select_fusion
  1.5 0.6 gather_fusion
  2.1 0.7 compare_and_fusion
  2.8 0.1 select_bitcast_fusion
  2.9 0.1 copy.12
  2.9 0.7 %convert_element_type.23 = f32[32,128]{1,0:T(8,128)S(1)} convert(bf16[32,128]{1,0:T(8,128)(2,1)} %param.13) | non-fusion elementwise | flops 4096 | bytes 24576 | tf_op jit(solution)/shard_map/convert_element_type | solution.py:52
  3.7 2.1 %fusion.7 = bf16[40,32,8]{1,2,0:T(8,128)(2,1)S(1)} fusion(f32[32,128]{1,0:T(8,128)S(1)} %convert_element_type.23, f32[40,128]{1,0:T(8,128)S(1)} %copy.12, s32[128]{0:T(128)} %param.15), kind=kOutput, calls=%fused_computation.9 | convolution fusion | flops 15893504 | bytes 57856 | tf_op jit(solution)/shard_map/skj,ja->ska/dot_general | solution.py:17
  5.8 0.1 copy.13
  5.9 0.0 copy-start.6
  5.9 0.0 copy-start.3
  6.0 0.0 copy-start.1
  6.0 26.2 %all_gather.9 = bf16[40,32,128]{0,1,2:T(8,128)(2,1)S(1)} all-gather(bf16[40,32,8]{0,1,2:T(8,128)(2,1)S(1)} %copy.13), channel_id=1, replica_groups=mesh['mp'=2,'row'=16] {'row'}, dimensions={2}, use_global_device_ids=true | all-gather | bytes 348160 | tf_op jit(solution)/shard_map/all_gather | solution.py:32
  32.2 0.0 copy-start
  32.2 1.4 %copy.14 = bf16[40,32,128]{2,1,0:T(8,128)(2,1)S(1)} copy(bf16[40,32,128]{0,1,2:T(8,128)(2,1)S(1)} %all_gather.9) | data formatting | bytes 655360 | tf_op jit(solution)/shard_map/all_gather | solution.py:32
  33.6 0.0 copy-done.6
  33.6 0.6 dynamic-slice
  34.8 0.0 copy-done.3
  34.8 0.2 dynamic-update-slice
  35.1 6.8 %all-reduce = s32[128]{0:T(128)S(1)} all-reduce(s32[128]{0:T(128)S(1)} %dynamic-update-slice), channel_id=1, replica_groups=mesh['mp'=2,'row'=16] {'row'}, use_global_device_ids=true, to_apply=%add | all-reduce | flops 128 | bytes 1024
  41.8 0.1 subtract_abs_fusion
  41.9 0.0 copy-done.1
  41.9 23.5 %all_gather.11 = bf16[128,1024]{1,0:T(8,128)(2,1)S(1)} all-gather(bf16[8,1024]{1,0:T(8,128)(2,1)S(1)} %copy-done.1), channel_id=1, replica_groups=mesh['mp'=2,'row'=16] {'row'}, dimensions={0}, use_global_device_ids=true | all-gather | bytes 278528 | tf_op jit(solution)/shard_map/all_gather | solution.py:39
  65.5 0.0 copy-done
  65.5 0.0 copy-start.2
  65.5 0.0 copy-start.4
  65.5 0.8 %fusion.2 = f32[40,32,8]{1,2,0:T(8,128)S(1)} fusion(bf16[40,32,128]{2,1,0:T(8,128)(2,1)S(1)} %copy.14, f32[40,1024]{1,0:T(8,128)S(1)} %convert_element_type.26, f32[8,1024]{1,0:T(8,128)S(1)} %convert_element_type.25, bf16[128,1024]{1,0:T(8,128)(2,1)S(1)} %all_gather.11, s32[8,128]{1,0:T(8,128)S(1)} %get-tuple-element.7, s32[8,128]{1,0:T(8,128)S(1)} %get-tuple-element.6), kind=kOutput, calls=%fused_computation.6 | convolution fusion | flops 87941120 | bytes 835584 | tf_op jit(solution)/shard_map/sab,skb->ska/dot_general | solution.py:48
  66.3 0.0 copy-done.5
  66.3 0.7 %fusion = f32[32,128]{1,0:T(8,128)S(1)} fusion(f32[40,32,8]{1,2,0:T(8,128)S(1)} %fusion.2, f32[40,128]{1,0:T(8,128)S(1)} %copy.12, s32[128]{0:T(128)S(1)} %copy-done.5), kind=kOutput, calls=%fused_computation.3 | convolution fusion | flops 16053248 | bytes 78336 | tf_op jit(solution)/shard_map/ska,ai->ski/dot_general | solution.py:51
  67.1 0.0 copy-done.2
  67.1 0.0 copy-done.4
  67.1 0.6 multiply_add_fusion
  (5 shorter events, 0.0 us)
Async XLA Ops:
  5.9 27.7 %copy-start.6 = (u32[32]{0:T(128)S(1)}, u32[32]{0:T(128)}, u32[]{:S(2)}) copy-start(u32[32]{0:T(128)} %constant.32) | copy-start | bytes 388
  5.9 28.9 %copy-start.3 = (s32[8]{0:T(128)S(1)}, s32[8]{0:T(128)}, u32[]{:S(2)}) copy-start(s32[8]{0:T(128)} %param.16) | copy-start | bytes 100
  6.0 36.0 %copy-start.1 = (bf16[8,1024]{1,0:T(8,128)(2,1)S(1)}, bf16[8,1024]{1,0:T(8,128)(2,1)}, u32[]{:S(2)}) copy-start(bf16[8,1024]{1,0:T(8,128)(2,1)} %param.10) | copy-start | bytes 49156
  32.2 33.3 %copy-start = (bf16[40,1024]{1,0:T(8,128)(2,1)S(1)}, bf16[40,1024]{1,0:T(8,128)(2,1)}, u32[]{:S(2)}) copy-start(bf16[40,1024]{1,0:T(8,128)(2,1)} %param.11) | copy-start | bytes 245764
  65.5 0.9 %copy-start.5 = (s32[128]{0:T(128)S(1)}, s32[128]{0:T(128)}, u32[]{:S(2)}) copy-start(s32[128]{0:T(128)} %param.15) | copy-start | bytes 1540
  65.5 1.6 %copy-start.2 = (bf16[32,128]{1,0:T(8,128)(2,1)S(1)}, bf16[32,128]{1,0:T(8,128)(2,1)}, u32[]{:S(2)}) copy-start(bf16[32,128]{1,0:T(8,128)(2,1)} %param.13) | copy-start | bytes 24580
  65.5 1.6 %copy-start.4 = (f32[128]{0:T(128)S(1)}, f32[128]{0:T(128)}, u32[]{:S(2)}) copy-start(f32[128]{0:T(128)} %param.17) | copy-start | bytes 1540
where the time goes:
time: 68 us; the launch traced here: 67.7 us
  blocking collectives  56.5 us (83%)
  local copies, waits for them, and re-layouts  3.89 us (6%)
  matrix products  3.68 us (5%)
  other arithmetic  2.84 us (4%)
  between operations  0.79 us (1%)
    all_gather x1, blocking collectives, local(): lax.all_gather(own_part, 'row', axis=2, tiled=True)  26.2 us
    all_gather x1, blocking collectives, local(): fetched = lax.all_gather(radial_funcs, 'row', axis=0, tiled=True)  23.5 us
    unnamed x1, blocking collectives  6.75 us
    dot_general x1, matrix products, project(): jnp.einsum('skj,ja->ska', scaled, member, precision=lax.Precision.HIGHEST)  2.11 us
    unnamed x17, local copies, waits for them, and re-layouts  1.69 us

commit v1 on v0

--- a/solution.py
+++ b/solution.py
@@ -36,7 +36,16 @@
         radial_funcs.astype(jnp.float32)[None] * kernels.astype(jnp.float32)[:, None, :]
     ).astype(jnp.bfloat16)
     weighted = weighted.reshape(num_degree * mult_dev, radial_funcs.shape[1])
-    fetched = lax.all_gather(radial_funcs, "row", axis=0, tiled=True)
+    ways = lax.axis_size("row")
+    up = [(d, (d + 1) % ways) for d in range(ways)]
+    down = [(d, (d - 1) % ways) for d in range(ways)]
+    earlier, later = ([radial_funcs], [radial_funcs])
+    for _ in range(ways // 2):
+        earlier.append(lax.ppermute(earlier[-1], "row", up))
+    for _ in range((ways - 1) // 2):
+        later.append(lax.ppermute(later[-1], "row", down))
+    line = jnp.concatenate([*earlier[::-1], *later[1:]], axis=0)
+    fetched = jnp.roll(line, (lax.axis_index("row") - ways // 2) * radial_funcs.shape[0], axis=0)
     piece_rows = fetched.shape[0]
     integral = lax.dot_general(
         weighted, fetched, (((1,), (1,)), ((), ())), preferred_element_type=jnp.float32

time: 68 us -> 82.2 us (1.21)
  starting transfers between devices: 0 us -> 25.7 us
  blocking collectives: 56.5 us -> 33.2 us
  waiting for transfers between devices: 0 us -> 9.59 us
  local copies, waits for them, and re-layouts: 3.89 us -> 5.26 us
    ppermute x0 -> x15, starting transfers between devices: none -> 25.7 us  [the longest x7 24.7 us: local(): later.append(lax.ppermute(later[-1], 'row', down))]
    all_gather x1 -> x0, blocking collectives: 23.5 us -> none  [local(): fetched = lax.all_gather(radial_funcs, 'row', axis=0, tiled=True)]
    ppermute x0 -> x15, waiting for transfers between devices: none -> 9.59 us  [the longest x8 7.65 us: local(): earlier.append(lax.ppermute(earlier[-1], 'row', up))]
    unnamed x1, blocking collectives: 6.75 us -> 12.1 us
    all_gather x1, blocking collectives: 26.2 us -> 21.1 us  [local(): lax.all_gather(own_part, 'row', axis=2, tiled=True)]
    unnamed x17 -> x43, local copies, waits for them, and re-layouts: 1.69 us -> 3.07 us
  transfers between devices with their start and end apart: 0 -> 15, of which waited for: 0 -> 7; matrix products, arithmetic and copies ran while one was open for 0% -> 12% of each run, Pallas kernels for 0% -> 0%
where the time goes in v1:
time: 82.2 us; the launch traced here: 81.9 us
  blocking collectives  33.2 us (40%)
  starting transfers between devices  25.7 us (31%)
  waiting for transfers between devices  9.59 us (12%)
  local copies, waits for them, and re-layouts  5.26 us (6%)
  matrix products  3.69 us (4%)
  other arithmetic  3.47 us (4%)
  between operations  1.03 us (1%)
    ppermute x7, starting transfers between devices, local(): later.append(lax.ppermute(later[-1], 'row', down))  24.7 us
    all_gather x1, blocking collectives, local(): lax.all_gather(own_part, 'row', axis=2, tiled=True)  21.1 us
    unnamed x1, blocking collectives  12.1 us
    ppermute x8, waiting for transfers between devices, local(): earlier.append(lax.ppermute(earlier[-1], 'row', up))  7.65 us
    unnamed x43, local copies, waits for them, and re-layouts  3.07 us
    dot_general x1, matrix products, project(): jnp.einsum('skj,ja->ska', scaled, member, precision=lax.Precision.HIGHEST)  2.11 us
    ppermute x7, waiting for transfers between devices, local(): later.append(lax.ppermute(later[-1], 'row', down))  1.94 us
  transfers between devices with their start and end apart: 15, of which 7 were waited for; matrix products, arithmetic and copies ran while one was open for 12% of the time, Pallas kernels for 0%

profile of v1, /device:TPU:0, one launch (start us, length us, event | category | flops | bytes accessed | tf_op | source)
XLA Modules:
  0.0 81.9 jit_solution(17248213298762119469)
XLA Ops:
  0.0 0.5 collective-permute-start
  0.5 5.0 %collective-permute-start.8 = (bf16[8,1024]{1,0:T(8,128)(2,1)}, bf16[8,1024]{1,0:T(8,128)(2,1)S(1)}, u32[]{:S(2)}, u32[]{:S(2)}) collective-permute-start(bf16[8,1024]{1,0:T(8,128)(2,1)} %param.10), channel_id=1, source_target_pairs={{0,15},{1,0},{2,1},{3,2},{4,3},{5,4},{6,5},{7,6},{8,7},{9,8},{10,9... | collective-permute-start | bytes 49160 | tf_op jit(solution)/shard_map/ppermute | solution.py:46
  5.4 1.6 %collective-permute-done = bf16[8,1024]{1,0:T(8,128)(2,1)S(1)} collective-permute-done((bf16[8,1024]{1,0:T(8,128)(2,1)}, bf16[8,1024]{1,0:T(8,128)(2,1)S(1)}, u32[]{:S(2)}, u32[]{:S(2)}) %collective-permute-start) | collective-permute-done | bytes 16416 | tf_op jit(solution)/shard_map/ppermute | solution.py:44
  7.1 0.7 compare_select_fusion
  7.7 5.2 %collective-permute-done.1 = bf16[8,1024]{1,0:T(8,128)(2,1)S(1)} collective-permute-done((bf16[8,1024]{1,0:T(8,128)(2,1)S(1)}, bf16[8,1024]{1,0:T(8,128)(2,1)S(1)}, u32[]{:S(2)}, u32[]{:S(2)}) %collective-permute-start.1) | collective-permute-done | bytes 16416 | tf_op jit(solution)/shard_map/ppermute | solution.py:44
  12.9 0.7 compare_and_fusion
  13.6 4.4 %collective-permute-start.9 = (bf16[8,1024]{1,0:T(8,128)(2,1)S(1)}, bf16[8,1024]{1,0:T(8,128)(2,1)S(1)}, u32[]{:S(2)}, u32[]{:S(2)}) collective-permute-start(bf16[8,1024]{1,0:T(8,128)(2,1)S(1)} %collective-permute-done.8), channel_id=1, source_target_pairs={{0,15},{1,0},{2,1},{3,2},{4,3},{5,4},{6,5},{7,6},{8,7},{9,8},{10,9... | collective-permute-start | bytes 49160 | tf_op jit(solution)/shard_map/ppermute | solution.py:46
  18.0 0.8 collective-permute-done.2
  18.8 0.8 %copy.11 = f32[40,128]{0,1:T(8,128)S(1)} copy(f32[40,128]{1,0:T(8,128)} %param.12) | data formatting | bytes 40960 | tf_op args[2]
  19.6 0.6 gather_fusion
  20.3 4.5 %collective-permute-start.10 = (bf16[8,1024]{1,0:T(8,128)(2,1)S(1)}, bf16[8,1024]{1,0:T(8,128)(2,1)S(1)}, u32[]{:S(2)}, u32[]{:S(2)}) collective-permute-start(bf16[8,1024]{1,0:T(8,128)(2,1)S(1)} %collective-permute-done.9), channel_id=1, source_target_pairs={{0,15},{1,0},{2,1},{3,2},{4,3},{5,4},{6,5},{7,6},{8,7},{9,8},{10,9... | collective-permute-start | bytes 49160 | tf_op jit(solution)/shard_map/ppermute | solution.py:46
  24.8 0.1 select_bitcast_fusion
  24.9 0.7 convert_element_type.23
  25.6 0.6 collective-permute-done.10
  26.2 4.4 %collective-permute-start.11 = (bf16[8,1024]{1,0:T(8,128)(2,1)S(1)}, bf16[8,1024]{1,0:T(8,128)(2,1)S(1)}, u32[]{:S(2)}, u32[]{:S(2)}) collective-permute-start(bf16[8,1024]{1,0:T(8,128)(2,1)S(1)} %collective-permute-done.10), channel_id=1, source_target_pairs={{0,15},{1,0},{2,1},{3,2},{4,3},{5,4},{6,5},{7,6},{8,7},{9,8},{10,9... | collective-permute-start | bytes 49160 | tf_op jit(solution)/shard_map/ppermute | solution.py:46
  30.6 2.1 %fusion.7 = bf16[40,32,8]{1,2,0:T(8,128)(2,1)S(1)} fusion(f32[32,128]{1,0:T(8,128)S(1)} %convert_element_type.23, f32[40,128]{1,0:T(8,128)S(1)} %copy.12, s32[128]{0:T(128)} %param.15), kind=kOutput, calls=%fused_computation.9 | convolution fusion | flops 15893504 | bytes 57856 | tf_op jit(solution)/shard_map/skj,ja->ska/dot_general | solution.py:17
  32.8 1.3 %dynamic-slice = u32[1]{0:T(128)} dynamic-slice(u32[32]{0:T(128)} %constant.61, u32[]{:T(128)S(6)} %add.55), dynamic_slice_sizes={1} | dynamic-slice | bytes 12
  34.7 0.9 %dynamic-update-slice = s32[128]{0:T(128)S(1)} dynamic-update-slice(s32[128]{0:T(128)S(1)} %lt.27, s32[8]{0:T(128)} %param.16, u32[]{:T(128)} %bitcast.2) | dynamic-update-slice | bytes 68
  35.5 12.1 %all-reduce = s32[128]{0:T(128)S(1)} all-reduce(s32[128]{0:T(128)S(1)} %dynamic-update-slice), channel_id=1, replica_groups=mesh['mp'=2,'row'=16] {'row'}, use_global_device_ids=true, to_apply=%add | all-reduce | flops 128 | bytes 1024
  47.6 0.5 collective-permute-start.6
  48.1 0.7 subtract_abs_fusion
  48.9 0.1 copy.13
  49.0 0.1 collective-permute-done.12
  49.1 4.4 %collective-permute-start.13 = (bf16[8,1024]{1,0:T(8,128)(2,1)S(1)}, bf16[8,1024]{1,0:T(8,128)(2,1)S(1)}, u32[]{:S(2)}, u32[]{:S(2)}) collective-permute-start(bf16[8,1024]{1,0:T(8,128)(2,1)S(1)} %collective-permute-done.12), channel_id=1, source_target_pairs={{0,15},{1,0},{2,1},{3,2},{4,3},{5,4},{6,5},{7,6},{8,7},{9,8},{10,9... | collective-permute-start | bytes 49160 | tf_op jit(solution)/shard_map/ppermute | solution.py:46
  53.5 0.1 collective-permute-done.6
  53.5 21.1 %all_gather.6 = bf16[40,32,128]{0,1,2:T(8,128)(2,1)S(1)} all-gather(bf16[40,32,8]{0,1,2:T(8,128)(2,1)S(1)} %copy.13), channel_id=1, replica_groups=mesh['mp'=2,'row'=16] {'row'}, dimensions={2}, use_global_device_ids=true | all-gather | bytes 348160 | tf_op jit(solution)/shard_map/all_gather | solution.py:32
  74.6 1.4 %copy.14 = bf16[40,32,128]{2,1,0:T(8,128)(2,1)S(1)} copy(bf16[40,32,128]{0,1,2:T(8,128)(2,1)S(1)} %all_gather.6) | data formatting | bytes 655360 | tf_op jit(solution)/shard_map/all_gather | solution.py:32
  76.1 2.0 %collective-permute-start.14 = (bf16[8,1024]{1,0:T(8,128)(2,1)S(1)}, bf16[8,1024]{1,0:T(8,128)(2,1)S(1)}, u32[]{:S(2)}, u32[]{:S(2)}) collective-permute-start(bf16[8,1024]{1,0:T(8,128)(2,1)S(1)} %collective-permute-done.13), channel_id=1, source_target_pairs={{0,15},{1,0},{2,1},{3,2},{4,3},{5,4},{6,5},{7,6},{8,7},{9,8},{10,9... | collective-permute-start | bytes 49160 | tf_op jit(solution)/shard_map/ppermute | solution.py:46
  78.2 1.3 %collective-permute-done.14 = bf16[8,1024]{1,0:T(8,128)(2,1)S(1)} collective-permute-done((bf16[8,1024]{1,0:T(8,128)(2,1)S(1)}, bf16[8,1024]{1,0:T(8,128)(2,1)S(1)}, u32[]{:S(2)}, u32[]{:S(2)}) %collective-permute-start.14) | collective-permute-done | bytes 16416 | tf_op jit(solution)/shard_map/ppermute | solution.py:46
  79.7 0.8 %fusion.2 = f32[40,32,8]{1,2,0:T(8,128)S(1)} fusion(bf16[40,32,128]{2,1,0:T(8,128)(2,1)S(1)} %copy.14, f32[40,1024]{1,0:T(8,128)S(1)} %convert_element_type.26, f32[8,1024]{1,0:T(8,128)S(1)} %get-tuple-element.7, bf16[256,1024]{1,0:T(8,128)(2,1)S(1)} %constant_dynamic-update-slice_fusion, s32[]{:T(128)S(6)} %select_n.32, s32[8,128]{1,0:T(8,128)S(1)} %get-tuple-element.9, ...), kind=kOutput, calls=%fused_computation.6 | convolution fusion | flops 87941120 | bytes 835588 | tf_op jit(solution)/shard_map/sab,skb->ska/dot_general | solution.py:57
  80.5 0.7 fusion
  81.3 0.6 multiply_add_fusion
  (61 shorter events, 0.3 us)
Async XLA Ops:
  0.0 7.1 %collective-permute-start = (bf16[8,1024]{1,0:T(8,128)(2,1)}, bf16[8,1024]{1,0:T(8,128)(2,1)S(1)}, u32[]{:S(2)}, u32[]{:S(2)}) collective-permute-start(bf16[8,1024]{1,0:T(8,128)(2,1)} %param.10), channel_id=1, source_target_pairs={{0,1},{1,2},{2,3},{3,4},{4,5},{5,6},{6,7},{7,8},{8,9},{9,10},{10,1... | collective-permute-start | bytes 49160 | tf_op jit(solution)/shard_map/ppermute | solution.py:44
  0.5 13.2 %collective-permute-start.8 = (bf16[8,1024]{1,0:T(8,128)(2,1)}, bf16[8,1024]{1,0:T(8,128)(2,1)S(1)}, u32[]{:S(2)}, u32[]{:S(2)}) collective-permute-start(bf16[8,1024]{1,0:T(8,128)(2,1)} %param.10), channel_id=1, source_target_pairs={{0,15},{1,0},{2,1},{3,2},{4,3},{5,4},{6,5},{7,6},{8,7},{9,8},{10,9... | collective-permute-start | bytes 49160 | tf_op jit(solution)/shard_map/ppermute | solution.py:46
  7.1 5.9 %collective-permute-start.1 = (bf16[8,1024]{1,0:T(8,128)(2,1)S(1)}, bf16[8,1024]{1,0:T(8,128)(2,1)S(1)}, u32[]{:S(2)}, u32[]{:S(2)}) collective-permute-start(bf16[8,1024]{1,0:T(8,128)(2,1)S(1)} %collective-permute-done), channel_id=1, source_target_pairs={{0,1},{1,2},{2,3},{3,4},{4,5},{5,6},{6,7},{7,8},{8,9},{9,10},{10,1... | collective-permute-start | bytes 49160 | tf_op jit(solution)/shard_map/ppermute | solution.py:44
  12.9 5.9 %collective-permute-start.2 = (bf16[8,1024]{1,0:T(8,128)(2,1)S(1)}, bf16[8,1024]{1,0:T(8,128)(2,1)S(1)}, u32[]{:S(2)}, u32[]{:S(2)}) collective-permute-start(bf16[8,1024]{1,0:T(8,128)(2,1)S(1)} %collective-permute-done.1), channel_id=1, source_target_pairs={{0,1},{1,2},{2,3},{3,4},{4,5},{5,6},{6,7},{7,8},{8,9},{9,10},{10,1... | collective-permute-start | bytes 49160 | tf_op jit(solution)/shard_map/ppermute | solution.py:44
  13.6 6.7 %collective-permute-start.9 = (bf16[8,1024]{1,0:T(8,128)(2,1)S(1)}, bf16[8,1024]{1,0:T(8,128)(2,1)S(1)}, u32[]{:S(2)}, u32[]{:S(2)}) collective-permute-start(bf16[8,1024]{1,0:T(8,128)(2,1)S(1)} %collective-permute-done.8), channel_id=1, source_target_pairs={{0,15},{1,0},{2,1},{3,2},{4,3},{5,4},{6,5},{7,6},{8,7},{9,8},{10,9... | collective-permute-start | bytes 49160 | tf_op jit(solution)/shard_map/ppermute | solution.py:46
  18.8 6.0 %collective-permute-start.3 = (bf16[8,1024]{1,0:T(8,128)(2,1)S(1)}, bf16[8,1024]{1,0:T(8,128)(2,1)S(1)}, u32[]{:S(2)}, u32[]{:S(2)}) collective-permute-start(bf16[8,1024]{1,0:T(8,128)(2,1)S(1)} %collective-permute-done.2), channel_id=1, source_target_pairs={{0,1},{1,2},{2,3},{3,4},{4,5},{5,6},{6,7},{7,8},{8,9},{9,10},{10,1... | collective-permute-start | bytes 49160 | tf_op jit(solution)/shard_map/ppermute | solution.py:44
  20.3 5.9 %collective-permute-start.10 = (bf16[8,1024]{1,0:T(8,128)(2,1)S(1)}, bf16[8,1024]{1,0:T(8,128)(2,1)S(1)}, u32[]{:S(2)}, u32[]{:S(2)}) collective-permute-start(bf16[8,1024]{1,0:T(8,128)(2,1)S(1)} %collective-permute-done.9), channel_id=1, source_target_pairs={{0,15},{1,0},{2,1},{3,2},{4,3},{5,4},{6,5},{7,6},{8,7},{9,8},{10,9... | collective-permute-start | bytes 49160 | tf_op jit(solution)/shard_map/ppermute | solution.py:46
  24.8 5.9 %collective-permute-start.4 = (bf16[8,1024]{1,0:T(8,128)(2,1)S(1)}, bf16[8,1024]{1,0:T(8,128)(2,1)S(1)}, u32[]{:S(2)}, u32[]{:S(2)}) collective-permute-start(bf16[8,1024]{1,0:T(8,128)(2,1)S(1)} %collective-permute-done.3), channel_id=1, source_target_pairs={{0,1},{1,2},{2,3},{3,4},{4,5},{5,6},{6,7},{7,8},{8,9},{9,10},{10,1... | collective-permute-start | bytes 49160 | tf_op jit(solution)/shard_map/ppermute | solution.py:44
  26.2 21.4 %collective-permute-start.11 = (bf16[8,1024]{1,0:T(8,128)(2,1)S(1)}, bf16[8,1024]{1,0:T(8,128)(2,1)S(1)}, u32[]{:S(2)}, u32[]{:S(2)}) collective-permute-start(bf16[8,1024]{1,0:T(8,128)(2,1)S(1)} %collective-permute-done.10), channel_id=1, source_target_pairs={{0,15},{1,0},{2,1},{3,2},{4,3},{5,4},{6,5},{7,6},{8,7},{9,8},{10,9... | collective-permute-start | bytes 49160 | tf_op jit(solution)/shard_map/ppermute | solution.py:46
  30.6 17.0 %collective-permute-start.5 = (bf16[8,1024]{1,0:T(8,128)(2,1)S(1)}, bf16[8,1024]{1,0:T(8,128)(2,1)S(1)}, u32[]{:S(2)}, u32[]{:S(2)}) collective-permute-start(bf16[8,1024]{1,0:T(8,128)(2,1)S(1)} %collective-permute-done.4), channel_id=1, source_target_pairs={{0,1},{1,2},{2,3},{3,4},{4,5},{5,6},{6,7},{7,8},{8,9},{9,10},{10,1... | collective-permute-start | bytes 49160 | tf_op jit(solution)/shard_map/ppermute | solution.py:44
  47.6 1.4 %collective-permute-start.12 = (bf16[8,1024]{1,0:T(8,128)(2,1)S(1)}, bf16[8,1024]{1,0:T(8,128)(2,1)S(1)}, u32[]{:S(2)}, u32[]{:S(2)}) collective-permute-start(bf16[8,1024]{1,0:T(8,128)(2,1)S(1)} %collective-permute-done.11), channel_id=1, source_target_pairs={{0,15},{1,0},{2,1},{3,2},{4,3},{5,4},{6,5},{7,6},{8,7},{9,8},{10,9... | collective-permute-start | bytes 49160 | tf_op jit(solution)/shard_map/ppermute | solution.py:46
  47.6 5.9 %collective-permute-start.6 = (bf16[8,1024]{1,0:T(8,128)(2,1)S(1)}, bf16[8,1024]{1,0:T(8,128)(2,1)S(1)}, u32[]{:S(2)}, u32[]{:S(2)}) collective-permute-start(bf16[8,1024]{1,0:T(8,128)(2,1)S(1)} %collective-permute-done.5), channel_id=1, source_target_pairs={{0,1},{1,2},{2,3},{3,4},{4,5},{5,6},{6,7},{7,8},{8,9},{9,10},{10,1... | collective-permute-start | bytes 49160 | tf_op jit(solution)/shard_map/ppermute | solution.py:44
  49.0 27.0 %copy-start = (bf16[40,1024]{1,0:T(8,128)(2,1)S(1)}, bf16[40,1024]{1,0:T(8,128)(2,1)}, u32[]{:S(2)}) copy-start(bf16[40,1024]{1,0:T(8,128)(2,1)} %param.11) | copy-start | bytes 245764
  49.1 27.0 %collective-permute-start.13 = (bf16[8,1024]{1,0:T(8,128)(2,1)S(1)}, bf16[8,1024]{1,0:T(8,128)(2,1)S(1)}, u32[]{:S(2)}, u32[]{:S(2)}) collective-permute-start(bf16[8,1024]{1,0:T(8,128)(2,1)S(1)} %collective-permute-done.12), channel_id=1, source_target_pairs={{0,15},{1,0},{2,1},{3,2},{4,3},{5,4},{6,5},{7,6},{8,7},{9,8},{10,9... | collective-permute-start | bytes 49160 | tf_op jit(solution)/shard_map/ppermute | solution.py:46
  53.5 24.5 %collective-permute-start.7 = (bf16[8,1024]{1,0:T(8,128)(2,1)S(1)}, bf16[8,1024]{1,0:T(8,128)(2,1)S(1)}, u32[]{:S(2)}, u32[]{:S(2)}) collective-permute-start(bf16[8,1024]{1,0:T(8,128)(2,1)S(1)} %collective-permute-done.6), channel_id=1, source_target_pairs={{0,1},{1,2},{2,3},{3,4},{4,5},{5,6},{6,7},{7,8},{8,9},{9,10},{10,1... | collective-permute-start | bytes 49160 | tf_op jit(solution)/shard_map/ppermute | solution.py:44
  74.6 3.5 %copy-start.1 = (bf16[8,1024]{1,0:T(8,128)(2,1)S(1)}, bf16[8,1024]{1,0:T(8,128)(2,1)}, u32[]{:S(2)}) copy-start(bf16[8,1024]{1,0:T(8,128)(2,1)} %param.10) | copy-start | bytes 49156
  76.1 3.4 %collective-permute-start.14 = (bf16[8,1024]{1,0:T(8,128)(2,1)S(1)}, bf16[8,1024]{1,0:T(8,128)(2,1)S(1)}, u32[]{:S(2)}, u32[]{:S(2)}) collective-permute-start(bf16[8,1024]{1,0:T(8,128)(2,1)S(1)} %collective-permute-done.13), channel_id=1, source_target_pairs={{0,15},{1,0},{2,1},{3,2},{4,3},{5,4},{6,5},{7,6},{8,7},{9,8},{10,9... | collective-permute-start | bytes 49160 | tf_op jit(solution)/shard_map/ppermute | solution.py:46
  79.6 0.9 %copy-start.4 = (s32[128]{0:T(128)S(1)}, s32[128]{0:T(128)}, u32[]{:S(2)}) copy-start(s32[128]{0:T(128)} %param.15) | copy-start | bytes 1540
  79.6 1.6 %copy-start.2 = (bf16[32,128]{1,0:T(8,128)(2,1)S(1)}, bf16[32,128]{1,0:T(8,128)(2,1)}, u32[]{:S(2)}) copy-start(bf16[32,128]{1,0:T(8,128)(2,1)} %param.13) | copy-start | bytes 24580
  79.7 1.6 %copy-start.3 = (f32[128]{0:T(128)S(1)}, f32[128]{0:T(128)}, u32[]{:S(2)}) copy-start(f32[128]{0:T(128)} %param.17) | copy-start | bytes 1540
